TPU v7x, 256 devices: a whole 4x4x8 slice. The times are simulated.
256 devices in a mesh: row: 32 (over z, x_hi, core), col: 8 (over y, x_lo).
Axes of the slice: x: 4 (x_hi: 2, x_lo: 2; x = x_hi * 2 + x_lo), y: 4, z: 8, core: 2. Of those that a mesh axis runs over, the one named last changes fastest.
Arguments:
- pair_map: bfloat16 [64, 1024, 1024], P(None, 'row', 'col'), may hold values from -6 to 6
- kernel_one_a: bfloat16 [3, 3, 64, 64], replicated, may hold values from -0.25 to 0.25
- bias_one_a: float32 [64], replicated, may hold values from -3 to 3
- kernel_one_b: bfloat16 [3, 3, 64, 64], replicated, may hold values from -0.25 to 0.25
- bias_one_b: float32 [64], replicated, may hold values from -3 to 3
- kernel_two_a: bfloat16 [3, 3, 64, 64], replicated, may hold values from -0.25 to 0.25
- bias_two_a: float32 [64], replicated, may hold values from -3 to 3
- kernel_two_b: bfloat16 [3, 3, 64, 64], replicated, may hold values from -0.25 to 0.25
- bias_two_b: float32 [64], replicated, may hold values from -3 to 3
Outputs:
- pair_out: bfloat16 [64, 1024, 1024], P(None, 'row', 'col')
All inputs are finite; a program needn't handle non-finite values.
Results may differ from a plain program's by a relative error of at most 0.0064.
Values may be sent and summed in bfloat16 or wider, within the bound.
A program may use at most 64 MiB of HBM per device.

v0:
```python
import jax
import jax.numpy as jnp
from jax import lax
from jax.sharding import PartitionSpec as P


def extended(shard, sides, width):
    for axis, dim in sides:
        size, length = (lax.axis_size(axis), shard.shape[dim])
        up = [(i, (i + 1) % size) for i in range(size - 1)]
        down = [(j, i) for i, j in up]
        last = lax.slice_in_dim(shard, length - width, length, axis=dim)
        initial = lax.slice_in_dim(shard, 0, width, axis=dim)
        before = lax.ppermute(last, axis, up)
        after = lax.ppermute(initial, axis, down)
        shard = jnp.concatenate([before, shard, after], axis=dim)
    return shard


def apply_dilated_conv(pair_field, filter_weight, dilation_rate):
    padded_input = extended(pair_field, (("row", 1), ("col", 2)), dilation_rate)
    map_height = pair_field.shape[1]
    map_width = pair_field.shape[2]
    taps = [
        padded_input[
            :,
            filter_row * dilation_rate : filter_row * dilation_rate + map_height,
            filter_column * dilation_rate : filter_column * dilation_rate + map_width,
        ]
        for filter_row in range(3)
        for filter_column in range(3)
    ]
    stacked = jnp.concatenate(taps, axis=0)
    flat_kernel = jnp.transpose(filter_weight, (2, 0, 1, 3)).reshape(filter_weight.shape[2], -1)
    return jnp.einsum("ok,kij->oij", flat_kernel, stacked, preferred_element_type=jnp.float32)


def mirrored(block_output):
    moved = lax.all_to_all(
        lax.all_to_all(block_output, "row", split_axis=0, concat_axis=1, tiled=True),
        "col",
        split_axis=1,
        concat_axis=2,
        tiled=True,
    )
    landed = lax.all_to_all(moved, "row", split_axis=2, concat_axis=0, tiled=True)
    return jnp.transpose(landed, (0, 2, 1))


def residual_block(source_map, first_filter, first_bias, second_filter, second_bias, dilation_rate):
    hidden_features = jax.nn.elu(
        apply_dilated_conv(source_map, first_filter, dilation_rate) + first_bias[:, None, None]
    ).astype(jnp.bfloat16)
    block_output = jax.nn.elu(
        source_map.astype(jnp.float32)
        + apply_dilated_conv(hidden_features, second_filter, dilation_rate)
        + second_bias[:, None, None]
    ).astype(jnp.bfloat16)
    mirror_tile = mirrored(block_output)
    return ((block_output.astype(jnp.float32) + mirror_tile.astype(jnp.float32)) * 0.5).astype(
        jnp.bfloat16
    )


def shards(
    pair_map,
    kernel_one_a,
    bias_one_a,
    kernel_one_b,
    bias_one_b,
    kernel_two_a,
    bias_two_a,
    kernel_two_b,
    bias_two_b,
):
    first = residual_block(pair_map, kernel_one_a, bias_one_a, kernel_one_b, bias_one_b, 2)
    return residual_block(first, kernel_two_a, bias_two_a, kernel_two_b, bias_two_b, 4)


def solution(mesh):
    placed = (P(None, "row", "col"), P(), P(), P(), P(), P(), P(), P(), P())
    return jax.shard_map(
        shards, mesh=mesh, in_specs=placed, out_specs=P(None, "row", "col"), check_vma=False
    )
```

profile of v0, /device:TPU:1, one launch (start us, length us, event | category | flops | bytes accessed | tf_op | source)
XLA Modules:
  0.0 245.4 jit_solution(1307448916431583036)
XLA Ops:
  0.0 1.3 copy.82
  1.3 6.0 %collective-permute-start = (bf16[64,2,128]{2,0,1:T(8,128)(2,1)S(1)}, bf16[64,2,128]{2,0,1:T(8,128)(2,1)S(1)}, u32[]{:S(2)}, u32[]{:S(2)}) collective-permute-start(bf16[64,2,128]{2,0,1:T(8,128)(2,1)S(1)} %get-tuple-element.26), channel_id=1, source_target_pairs={{0,8},{8,16},{16,24},{24,32},{32,40},{40,48},{48,56},{56,64},{64,7... | collective-permute-start | bytes 98312 | tf_op jit(solution)/shard_map/ppermute | solution.py:14
  7.4 1.9 collective-permute-start.1
  9.3 1.3 constant_dynamic-update-slice_fusion.1
  10.6 3.5 %collective-permute-done.1 = bf16[64,2,128]{2,0,1:T(8,128)(2,1)S(1)} collective-permute-done((bf16[64,2,128]{2,0,1:T(8,128)(2,1)S(1)}, bf16[64,2,128]{2,0,1:T(8,128)(2,1)S(1)}, u32[]{:S(2)}, u32[]{:S(2)}) %collective-permute-start.1) | collective-permute-done | bytes 32800 | tf_op jit(solution)/shard_map/ppermute | solution.py:15
  14.7 2.2 collective-permute-start.2
  17.4 1.3 collective-permute-start.3
  18.7 0.4 copy.87
  19.0 1.1 fusion.21
  20.2 0.9 fusion.31
  21.1 1.5 collective-permute-done.3
  22.6 0.4 copy.90
  23.0 1.2 fusion.17
  24.2 1.1 fusion.19
  25.3 1.0 constant_dynamic-update-slice_fusion.3
  26.3 1.2 fusion.15
  27.5 1.1 fusion.30
  28.6 0.9 fusion.29
  29.5 1.2 fusion.28
  30.7 3.7 %fusion.7 = bf16[64,32,128]{2,0,1:T(8,128)(2,1)S(1)} fusion(bf16[576,32,128]{2,0,1:T(8,128)(2,1)} %fusion.28, bf16[64,576,1]{0,1,2:T(8,128)(2,1)S(1)} %bitcast.102, f32[64]{0:T(128)S(1)} %copy-done.5), kind=kOutput, calls=%fused_computation.33 | convolution fusion | flops 303300608 | bytes 5316864 | tf_op jit(solution)/shard_map/ok,kij->oij/dot_general | solution.py:35
  34.5 3.2 %collective-permute-start.4 = (bf16[64,2,128]{2,0,1:T(8,128)(2,1)S(1)}, bf16[64,2,128]{2,0,1:T(8,128)(2,1)S(1)}, u32[]{:S(2)}, u32[]{:S(2)}) collective-permute-start(bf16[64,2,128]{2,0,1:T(8,128)(2,1)S(1)} %get-tuple-element.23), channel_id=1, source_target_pairs={{0,8},{8,16},{16,24},{24,32},{32,40},{40,48},{48,56},{56,64},{64,7... | collective-permute-start | bytes 98312 | tf_op jit(solution)/shard_map/ppermute | solution.py:14
  37.7 1.9 collective-permute-start.5
  39.6 4.8 %collective-permute-done.5 = bf16[64,2,128]{2,0,1:T(8,128)(2,1)S(1)} collective-permute-done((bf16[64,2,128]{2,0,1:T(8,128)(2,1)S(1)}, bf16[64,2,128]{2,0,1:T(8,128)(2,1)S(1)}, u32[]{:S(2)}, u32[]{:S(2)}) %collective-permute-start.5) | collective-permute-done | bytes 32800 | tf_op jit(solution)/shard_map/ppermute | solution.py:15
  45.1 3.8 %collective-permute-start.6 = (bf16[64,36,2]{0,2,1:T(2,128)(2,1)S(1)}, bf16[64,36,2]{0,2,1:T(2,128)(2,1)S(1)}, u32[]{:S(2)}, u32[]{:S(2)}) collective-permute-start(bf16[64,36,2]{0,2,1:T(2,128)(2,1)S(1)} %copy.95), channel_id=1, source_target_pairs={{0,1},{1,2},{2,3},{3,4},{4,5},{5,6},{6,7},{8,9},{9,10},{10,11},{11... | collective-permute-start | bytes 27656 | tf_op jit(solution)/shard_map/ppermute | solution.py:14
  49.2 1.3 collective-permute-start.7
  50.6 0.4 copy.96
  51.0 2.7 %collective-permute-done.7 = bf16[64,36,2]{0,2,1:T(2,128)(2,1)S(1)} collective-permute-done((bf16[64,36,2]{0,2,1:T(2,128)(2,1)S(1)}, bf16[64,36,2]{0,2,1:T(2,128)(2,1)S(1)}, u32[]{:S(2)}, u32[]{:S(2)}) %collective-permute-start.7) | collective-permute-done | bytes 9248 | tf_op jit(solution)/shard_map/ppermute | solution.py:15
  53.7 0.4 copy.98
  54.0 0.8 pad_maximum_fusion.2
  56.4 1.5 fusion.9
  57.9 0.3 copy.101
  58.2 31.0 %all_to_all.90 = bf16[64,32,128]{2,1,0:T(8,128)(2,1)S(1)} all-to-all(bf16[64,32,128]{2,1,0:T(8,128)(2,1)S(1)} %copy.101), channel_id=1, replica_groups=mesh['row'=32,'col'=8] {'row'}, dimensions={0} | all-to-all | bytes 1048576 | tf_op jit(solution)/shard_map/all_to_all | solution.py:40
  89.3 0.5 copy.103
  89.8 12.3 %all_to_all.91 = bf16[2,1024,128]{2,0,1:T(2,128)(2,1)S(1)} all-to-all(bf16[2,1024,128]{2,0,1:T(2,128)(2,1)S(1)} %copy.103), channel_id=1, replica_groups=mesh['row'=32,'col'=8] {'col'}, dimensions={1} | all-to-all | bytes 1048576 | tf_op jit(solution)/shard_map/all_to_all | solution.py:39
  102.5 0.5 copy.106
  103.0 24.7 %all_to_all.92 = bf16[2,128,1024]{1,0,2:T(2,128)(2,1)S(1)} all-to-all(bf16[2,128,1024]{1,0,2:T(2,128)(2,1)S(1)} %copy.106), channel_id=1, replica_groups=mesh['row'=32,'col'=8] {'row'}, dimensions={2} | all-to-all | bytes 1048576 | tf_op jit(solution)/shard_map/all_to_all | solution.py:46
  128.0 0.8 copy.108
  129.0 5.7 %collective-permute-start.8 = (bf16[64,4,128]{2,0,1:T(8,128)(2,1)S(1)}, bf16[64,4,128]{2,0,1:T(8,128)(2,1)S(1)}, u32[]{:S(2)}, u32[]{:S(2)}) collective-permute-start(bf16[64,4,128]{2,0,1:T(8,128)(2,1)S(1)} %get-tuple-element.21), channel_id=1, source_target_pairs={{0,8},{8,16},{16,24},{24,32},{32,40},{40,48},{48,56},{56,64},{64,7... | collective-permute-start | bytes 196616 | tf_op jit(solution)/shard_map/ppermute | solution.py:14
  134.8 1.9 collective-permute-start.9
  136.7 5.2 %collective-permute-done.9 = bf16[64,4,128]{2,0,1:T(8,128)(2,1)S(1)} collective-permute-done((bf16[64,4,128]{2,0,1:T(8,128)(2,1)S(1)}, bf16[64,4,128]{2,0,1:T(8,128)(2,1)S(1)}, u32[]{:S(2)}, u32[]{:S(2)}) %collective-permute-start.9) | collective-permute-done | bytes 65568 | tf_op jit(solution)/shard_map/ppermute | solution.py:15
  142.6 2.0 collective-permute-start.10
  144.9 1.3 collective-permute-start.11
  146.4 0.4 copy.110
  146.8 2.9 %collective-permute-done.11 = bf16[64,40,4]{0,1,2:T(8,128)(2,1)S(1)} collective-permute-done((bf16[64,40,4]{0,1,2:T(8,128)(2,1)S(1)}, bf16[64,40,4]{0,1,2:T(8,128)(2,1)S(1)}, u32[]{:S(2)}, u32[]{:S(2)}) %collective-permute-start.11) | collective-permute-done | bytes 20512 | tf_op jit(solution)/shard_map/ppermute | solution.py:15
  149.6 0.4 copy.112
  150.0 1.3 pad_maximum_fusion
  153.0 1.4 fusion.11
  154.4 3.9 %collective-permute-start.12 = (bf16[64,4,128]{2,0,1:T(8,128)(2,1)S(1)}, bf16[64,4,128]{2,0,1:T(8,128)(2,1)S(1)}, u32[]{:S(2)}, u32[]{:S(2)}) collective-permute-start(bf16[64,4,128]{2,0,1:T(8,128)(2,1)S(1)} %get-tuple-element.19), channel_id=1, source_target_pairs={{0,8},{8,16},{16,24},{24,32},{32,40},{40,48},{48,56},{56,64},{64,7... | collective-permute-start | bytes 196616 | tf_op jit(solution)/shard_map/ppermute | solution.py:14
  158.3 1.9 collective-permute-start.13
  160.2 5.2 %collective-permute-done.13 = bf16[64,4,128]{2,0,1:T(8,128)(2,1)S(1)} collective-permute-done((bf16[64,4,128]{2,0,1:T(8,128)(2,1)S(1)}, bf16[64,4,128]{2,0,1:T(8,128)(2,1)S(1)}, u32[]{:S(2)}, u32[]{:S(2)}) %collective-permute-start.13) | collective-permute-done | bytes 65568 | tf_op jit(solution)/shard_map/ppermute | solution.py:15
  166.1 2.7 %collective-permute-start.14 = (bf16[64,40,4]{0,1,2:T(8,128)(2,1)S(1)}, bf16[64,40,4]{0,1,2:T(8,128)(2,1)S(1)}, u32[]{:S(2)}, u32[]{:S(2)}) collective-permute-start(bf16[64,40,4]{0,1,2:T(8,128)(2,1)S(1)} %copy.115), channel_id=1, source_target_pairs={{0,1},{1,2},{2,3},{3,4},{4,5},{5,6},{6,7},{8,9},{9,10},{10,11},{11... | collective-permute-start | bytes 61448 | tf_op jit(solution)/shard_map/ppermute | solution.py:14
  169.1 1.5 collective-permute-start.15
  170.8 0.4 copy.116
  171.2 2.7 %collective-permute-done.15 = bf16[64,40,4]{0,1,2:T(8,128)(2,1)S(1)} collective-permute-done((bf16[64,40,4]{0,1,2:T(8,128)(2,1)S(1)}, bf16[64,40,4]{0,1,2:T(8,128)(2,1)S(1)}, u32[]{:S(2)}, u32[]{:S(2)}) %collective-permute-start.15) | collective-permute-done | bytes 20512 | tf_op jit(solution)/shard_map/ppermute | solution.py:15
  173.9 0.4 copy.118
  174.3 1.3 pad_maximum_fusion.1
  177.2 1.4 fusion.13
  179.0 26.3 %all_to_all.93 = bf16[64,32,128]{2,1,0:T(8,128)(2,1)S(1)} all-to-all(bf16[64,32,128]{2,1,0:T(8,128)(2,1)S(1)} %copy.121), channel_id=1, replica_groups=mesh['row'=32,'col'=8] {'row'}, dimensions={0} | all-to-all | bytes 1048576 | tf_op jit(solution)/shard_map/all_to_all | solution.py:40
  205.3 0.5 copy.123
  205.9 11.5 %all_to_all.94 = bf16[2,1024,128]{2,0,1:T(2,128)(2,1)S(1)} all-to-all(bf16[2,1024,128]{2,0,1:T(2,128)(2,1)S(1)} %copy.123), channel_id=1, replica_groups=mesh['row'=32,'col'=8] {'col'}, dimensions={1} | all-to-all | bytes 1048576 | tf_op jit(solution)/shard_map/all_to_all | solution.py:39
  217.7 0.5 copy.126
  218.3 24.7 %all_to_all.95 = bf16[2,128,1024]{1,0,2:T(2,128)(2,1)S(1)} all-to-all(bf16[2,128,1024]{1,0,2:T(2,128)(2,1)S(1)} %copy.126), channel_id=1, replica_groups=mesh['row'=32,'col'=8] {'row'}, dimensions={2} | all-to-all | bytes 1048576 | tf_op jit(solution)/shard_map/all_to_all | solution.py:46
  243.2 0.8 copy.128
  244.2 1.1 copy.129
  (91 shorter events, 10.9 us)
Async XLA Ops:
  0.0 16.9 %copy-start.1 = (bf16[3,3,64,64]{3,2,1,0:T(8,128)(2,1)S(1)}, bf16[3,3,64,64]{3,2,1,0:T(8,128)(2,1)}, u32[]{:S(2)}) copy-start(bf16[3,3,64,64]{3,2,1,0:T(8,128)(2,1)} %param.10) | copy-start | bytes 221188
  1.3 8.0 %collective-permute-start = (bf16[64,2,128]{2,0,1:T(8,128)(2,1)S(1)}, bf16[64,2,128]{2,0,1:T(8,128)(2,1)S(1)}, u32[]{:S(2)}, u32[]{:S(2)}) collective-permute-start(bf16[64,2,128]{2,0,1:T(8,128)(2,1)S(1)} %get-tuple-element.26), channel_id=1, source_target_pairs={{0,8},{8,16},{16,24},{24,32},{32,40},{40,48},{48,56},{56,64},{64,7... | collective-permute-start | bytes 98312 | tf_op jit(solution)/shard_map/ppermute | solution.py:14
  7.4 6.7 %collective-permute-start.1 = (bf16[64,2,128]{2,0,1:T(8,128)(2,1)S(1)}, bf16[64,2,128]{2,0,1:T(8,128)(2,1)S(1)}, u32[]{:S(2)}, u32[]{:S(2)}) collective-permute-start(bf16[64,2,128]{2,0,1:T(8,128)(2,1)S(1)} %get-tuple-element.25), channel_id=1, source_target_pairs={{8,0},{16,8},{24,16},{32,24},{40,32},{48,40},{56,48},{64,56},{72,6... | collective-permute-start | bytes 98312 | tf_op jit(solution)/shard_map/ppermute | solution.py:15
  14.4 10.9 %copy-start = (bf16[64,32,128]{2,1,0:T(8,128)(2,1)S(1)}, bf16[64,32,128]{2,1,0:T(8,128)(2,1)}, u32[]{:S(2)}) copy-start(bf16[64,32,128]{2,1,0:T(8,128)(2,1)} %param.9) | copy-start | bytes 1572868
  14.7 4.0 %collective-permute-start.2 = (bf16[64,36,2]{0,2,1:T(2,128)(2,1)S(1)}, bf16[64,36,2]{0,2,1:T(2,128)(2,1)S(1)}, u32[]{:S(2)}, u32[]{:S(2)}) collective-permute-start(bf16[64,36,2]{0,2,1:T(2,128)(2,1)S(1)} %copy.86), channel_id=1, source_target_pairs={{0,1},{1,2},{2,3},{3,4},{4,5},{5,6},{6,7},{8,9},{9,10},{10,11},{11... | collective-permute-start | bytes 27656 | tf_op jit(solution)/shard_map/ppermute | solution.py:14
  17.4 5.2 %collective-permute-start.3 = (bf16[64,36,2]{0,2,1:T(2,128)(2,1)S(1)}, bf16[64,36,2]{0,2,1:T(2,128)(2,1)S(1)}, u32[]{:S(2)}, u32[]{:S(2)}) collective-permute-start(bf16[64,36,2]{0,2,1:T(2,128)(2,1)S(1)} %copy.89), channel_id=1, source_target_pairs={{1,0},{2,1},{3,2},{4,3},{5,4},{6,5},{7,6},{9,8},{10,9},{11,10},{12... | collective-permute-start | bytes 27656 | tf_op jit(solution)/shard_map/ppermute | solution.py:15
  24.2 6.6 %copy-start.5 = (f32[64]{0:T(128)S(1)}, f32[64]{0:T(128)}, u32[]{:S(2)}) copy-start(f32[64]{0:T(128)} %param.11) | copy-start | bytes 772
  30.7 19.8 %copy-start.2 = (bf16[3,3,64,64]{3,2,1,0:T(8,128)(2,1)S(1)}, bf16[3,3,64,64]{3,2,1,0:T(8,128)(2,1)}, u32[]{:S(2)}) copy-start(bf16[3,3,64,64]{3,2,1,0:T(8,128)(2,1)} %param.12) | copy-start | bytes 221188
  34.5 5.2 %collective-permute-start.4 = (bf16[64,2,128]{2,0,1:T(8,128)(2,1)S(1)}, bf16[64,2,128]{2,0,1:T(8,128)(2,1)S(1)}, u32[]{:S(2)}, u32[]{:S(2)}) collective-permute-start(bf16[64,2,128]{2,0,1:T(8,128)(2,1)S(1)} %get-tuple-element.23), channel_id=1, source_target_pairs={{0,8},{8,16},{16,24},{24,32},{32,40},{40,48},{48,56},{56,64},{64,7... | collective-permute-start | bytes 98312 | tf_op jit(solution)/shard_map/ppermute | solution.py:14
  37.7 6.7 %collective-permute-start.5 = (bf16[64,2,128]{2,0,1:T(8,128)(2,1)S(1)}, bf16[64,2,128]{2,0,1:T(8,128)(2,1)S(1)}, u32[]{:S(2)}, u32[]{:S(2)}) collective-permute-start(bf16[64,2,128]{2,0,1:T(8,128)(2,1)S(1)} %get-tuple-element.24), channel_id=1, source_target_pairs={{8,0},{16,8},{24,16},{32,24},{40,32},{48,40},{56,48},{64,56},{72,6... | collective-permute-start | bytes 98312 | tf_op jit(solution)/shard_map/ppermute | solution.py:15
  45.1 5.5 %collective-permute-start.6 = (bf16[64,36,2]{0,2,1:T(2,128)(2,1)S(1)}, bf16[64,36,2]{0,2,1:T(2,128)(2,1)S(1)}, u32[]{:S(2)}, u32[]{:S(2)}) collective-permute-start(bf16[64,36,2]{0,2,1:T(2,128)(2,1)S(1)} %copy.95), channel_id=1, source_target_pairs={{0,1},{1,2},{2,3},{3,4},{4,5},{5,6},{6,7},{8,9},{9,10},{10,11},{11... | collective-permute-start | bytes 27656 | tf_op jit(solution)/shard_map/ppermute | solution.py:14
  49.2 4.5 %collective-permute-start.7 = (bf16[64,36,2]{0,2,1:T(2,128)(2,1)S(1)}, bf16[64,36,2]{0,2,1:T(2,128)(2,1)S(1)}, u32[]{:S(2)}, u32[]{:S(2)}) collective-permute-start(bf16[64,36,2]{0,2,1:T(2,128)(2,1)S(1)} %copy.97), channel_id=1, source_target_pairs={{1,0},{2,1},{3,2},{4,3},{5,4},{6,5},{7,6},{9,8},{10,9},{11,10},{12... | collective-permute-start | bytes 27656 | tf_op jit(solution)/shard_map/ppermute | solution.py:15
  54.9 1.5 copy-start.6
  128.0 18.2 %copy-start.3 = (bf16[3,3,64,64]{3,2,1,0:T(8,128)(2,1)S(1)}, bf16[3,3,64,64]{3,2,1,0:T(8,128)(2,1)}, u32[]{:S(2)}) copy-start(bf16[3,3,64,64]{3,2,1,0:T(8,128)(2,1)} %param.14) | copy-start | bytes 221188
  129.0 7.7 %collective-permute-start.8 = (bf16[64,4,128]{2,0,1:T(8,128)(2,1)S(1)}, bf16[64,4,128]{2,0,1:T(8,128)(2,1)S(1)}, u32[]{:S(2)}, u32[]{:S(2)}) collective-permute-start(bf16[64,4,128]{2,0,1:T(8,128)(2,1)S(1)} %get-tuple-element.21), channel_id=1, source_target_pairs={{0,8},{8,16},{16,24},{24,32},{32,40},{40,48},{48,56},{56,64},{64,7... | collective-permute-start | bytes 196616 | tf_op jit(solution)/shard_map/ppermute | solution.py:14
  134.8 7.1 %collective-permute-start.9 = (bf16[64,4,128]{2,0,1:T(8,128)(2,1)S(1)}, bf16[64,4,128]{2,0,1:T(8,128)(2,1)S(1)}, u32[]{:S(2)}, u32[]{:S(2)}) collective-permute-start(bf16[64,4,128]{2,0,1:T(8,128)(2,1)S(1)} %get-tuple-element.22), channel_id=1, source_target_pairs={{8,0},{16,8},{24,16},{32,24},{40,32},{48,40},{56,48},{64,56},{72,6... | collective-permute-start | bytes 196616 | tf_op jit(solution)/shard_map/ppermute | solution.py:15
  142.6 3.8 %collective-permute-start.10 = (bf16[64,40,4]{0,1,2:T(8,128)(2,1)S(1)}, bf16[64,40,4]{0,1,2:T(8,128)(2,1)S(1)}, u32[]{:S(2)}, u32[]{:S(2)}) collective-permute-start(bf16[64,40,4]{0,1,2:T(8,128)(2,1)S(1)} %copy.109), channel_id=1, source_target_pairs={{0,1},{1,2},{2,3},{3,4},{4,5},{5,6},{6,7},{8,9},{9,10},{10,11},{11... | collective-permute-start | bytes 61448 | tf_op jit(solution)/shard_map/ppermute | solution.py:14
  144.9 4.7 %collective-permute-start.11 = (bf16[64,40,4]{0,1,2:T(8,128)(2,1)S(1)}, bf16[64,40,4]{0,1,2:T(8,128)(2,1)S(1)}, u32[]{:S(2)}, u32[]{:S(2)}) collective-permute-start(bf16[64,40,4]{0,1,2:T(8,128)(2,1)S(1)} %copy.111), channel_id=1, source_target_pairs={{1,0},{2,1},{3,2},{4,3},{5,4},{6,5},{7,6},{9,8},{10,9},{11,10},{12... | collective-permute-start | bytes 61448 | tf_op jit(solution)/shard_map/ppermute | solution.py:15
  151.4 1.6 copy-start.7
  153.0 17.7 %copy-start.4 = (bf16[3,3,64,64]{3,2,1,0:T(8,128)(2,1)S(1)}, bf16[3,3,64,64]{3,2,1,0:T(8,128)(2,1)}, u32[]{:S(2)}) copy-start(bf16[3,3,64,64]{3,2,1,0:T(8,128)(2,1)} %param.16) | copy-start | bytes 221188
  154.4 5.8 %collective-permute-start.12 = (bf16[64,4,128]{2,0,1:T(8,128)(2,1)S(1)}, bf16[64,4,128]{2,0,1:T(8,128)(2,1)S(1)}, u32[]{:S(2)}, u32[]{:S(2)}) collective-permute-start(bf16[64,4,128]{2,0,1:T(8,128)(2,1)S(1)} %get-tuple-element.19), channel_id=1, source_target_pairs={{0,8},{8,16},{16,24},{24,32},{32,40},{40,48},{48,56},{56,64},{64,7... | collective-permute-start | bytes 196616 | tf_op jit(solution)/shard_map/ppermute | solution.py:14
  158.3 7.1 %collective-permute-start.13 = (bf16[64,4,128]{2,0,1:T(8,128)(2,1)S(1)}, bf16[64,4,128]{2,0,1:T(8,128)(2,1)S(1)}, u32[]{:S(2)}, u32[]{:S(2)}) collective-permute-start(bf16[64,4,128]{2,0,1:T(8,128)(2,1)S(1)} %get-tuple-element.20), channel_id=1, source_target_pairs={{8,0},{16,8},{24,16},{32,24},{40,32},{48,40},{56,48},{64,56},{72,6... | collective-permute-start | bytes 196616 | tf_op jit(solution)/shard_map/ppermute | solution.py:15
  166.1 4.7 %collective-permute-start.14 = (bf16[64,40,4]{0,1,2:T(8,128)(2,1)S(1)}, bf16[64,40,4]{0,1,2:T(8,128)(2,1)S(1)}, u32[]{:S(2)}, u32[]{:S(2)}) collective-permute-start(bf16[64,40,4]{0,1,2:T(8,128)(2,1)S(1)} %copy.115), channel_id=1, source_target_pairs={{0,1},{1,2},{2,3},{3,4},{4,5},{5,6},{6,7},{8,9},{9,10},{10,11},{11... | collective-permute-start | bytes 61448 | tf_op jit(solution)/shard_map/ppermute | solution.py:14
  169.1 4.7 %collective-permute-start.15 = (bf16[64,40,4]{0,1,2:T(8,128)(2,1)S(1)}, bf16[64,40,4]{0,1,2:T(8,128)(2,1)S(1)}, u32[]{:S(2)}, u32[]{:S(2)}) collective-permute-start(bf16[64,40,4]{0,1,2:T(8,128)(2,1)S(1)} %copy.117), channel_id=1, source_target_pairs={{1,0},{2,1},{3,2},{4,3},{5,4},{6,5},{7,6},{9,8},{10,9},{11,10},{12... | collective-permute-start | bytes 61448 | tf_op jit(solution)/shard_map/ppermute | solution.py:15
  175.6 1.6 copy-start.8
where the time goes:
time: 246 us; the launch traced here: 245 us
  blocking collectives  131 us (53%)
  starting transfers between devices  42.6 us (17%)
  waiting for transfers between devices  28.3 us (12%)
  local copies, waits for them, and re-layouts  21.5 us (9%)
  other arithmetic  13.6 us (6%)
  matrix products  7.99 us (3%)
    all_to_all x2, blocking collectives, mirrored(): lax.all_to_all(block_output, 'row', split_axis=0, concat_axis=1, tiled=True)  57.3 us
    all_to_all x2, blocking collectives, mirrored(): lax.all_to_all(moved, 'row', split_axis=2, concat_axis=0, tiled=True)  49.5 us
    ppermute x8, starting transfers between devices, extended(): before = lax.ppermute(last, axis, up)  29.5 us
    ppermute x8, waiting for transfers between devices, extended(): after = lax.ppermute(initial, axis, down)  28.3 us
    all_to_all x2, blocking collectives, mirrored(): lax.all_to_all(lax.all_to_all(block_output, 'row', split_axis=0, concat_a...  23.7 us
    ppermute x8, starting transfers between devices, extended(): after = lax.ppermute(initial, axis, down)  13.1 us
    dot_general x4, matrix products, apply_dilated_conv(): jnp.einsum('ok,kij->oij', flat_kernel, stacked, preferred_element_type=jn...  7.99 us
    unnamed x13, other arithmetic  7.99 us
  transfers between devices with their start and end apart: 16, of which 8 were waited for; matrix products, arithmetic and copies ran while one was open for 3% of the time, Pallas kernels for 0%

commit v1 on v0

v1 whole, which is shorter than its diff:
```python
import functools

import jax
import jax.numpy as jnp
from jax import lax
from jax.experimental import pallas as pl
from jax.experimental.pallas import tpu as pltpu
from jax.sharding import PartitionSpec as P

MESH = pl.DeviceIdType.MESH
F32, BF16 = jnp.float32, jnp.bfloat16
NT = (((1,), (1,)), ((), ()))
ROWS, COLS, CHAN, SIDE, QUAD = 32, 128, 64, 8, 4
ROW_PAD, COL_PAD, HID_ROW, HID_COL = 8, 16, 4, 8
NEIGHBOURS = [(dr, dc) for dr in (-1, 0, 1) for dc in (-1, 0, 1) if dr or dc]


def elu(v):
    return jnp.where(v > 0, v, jnp.exp(jnp.minimum(v, 0.0)) - 1.0)


def rounded(v):
    return v.astype(BF16).astype(F32)


def low_lanes(shape):
    return lax.broadcasted_iota(jnp.int32, shape, len(shape) - 1) < CHAN


def doubled(packed):
    turned = pltpu.roll(packed, CHAN, packed.ndim - 1)
    low = low_lanes(packed.shape)
    return jnp.where(low, packed, turned), jnp.where(low, turned, packed)


def paired(first, second):
    return jnp.where(low_lanes(first.shape), first, second)


class Halo:
    def __init__(self, rows, frame, send, recv, send_sem, recv_sem, row, col):
        self.rows, self.frame = rows, frame
        self.send, self.recv = send, recv
        self.send_sem, self.recv_sem = send_sem, recv_sem
        self.row, self.col = row, col

    def parts(self, at):
        dr, dc = NEIGHBOURS[at]
        if dc == 0:
            return 0 if dr < 0 else 1, self.rows * 4
        if dr == 0:
            return 2 if dc < 0 else 3, 8
        return 4 + (dr > 0) * 2 + (dc > 0), self.rows // 4

    def copy(self, at):
        dr, dc = NEIGHBOURS[at]
        there = len(NEIGHBOURS) - 1 - at
        mine, count = self.parts(at)
        other, _ = self.parts(there)
        device = (lax.rem(self.row + dr + 32, 32), lax.rem(self.col + dc + SIDE, SIDE))
        return pltpu.make_async_remote_copy(
            self.send.at[mine, pl.ds(0, count)],
            self.recv.at[other, pl.ds(0, count)],
            self.send_sem.at[mine],
            self.recv_sem.at[other],
            device_id=device,
            device_id_type=MESH,
        )

    def incoming(self, at):
        mine, count = self.parts(at)
        there = self.recv.at[mine, pl.ds(0, count)]
        return pltpu.make_async_copy(there, there, self.recv_sem.at[mine])

    def start(self):
        frame, rows = self.frame, self.rows
        for at, (dr, dc) in enumerate(NEIGHBOURS):
            mine, _ = self.parts(at)
            top = ROW_PAD if dr < 0 else ROW_PAD + ROWS - rows
            left = COL_PAD if dc < 0 else COL_PAD + COLS - 8
            if dc == 0:

                def pack_row(i, _, mine=mine, top=top):
                    line = frame[top + i, COL_PAD : COL_PAD + COLS, :]
                    both = paired(line[:64], line[64:]).astype(BF16)
                    self.send[mine, pl.ds(i * 4, 4)] = both.reshape(4, 16, 128)
                    return 0

                lax.fori_loop(0, rows, pack_row, 0)
            else:
                base, many = (ROW_PAD, ROWS // 4) if dr == 0 else (top, rows // 4)

                def pack_block(t, _, mine=mine, left=left, base=base):
                    block = frame[pl.ds(base + 4 * t, 4), left : left + 8, :]
                    both = paired(block[:2].reshape(16, 128), block[2:].reshape(16, 128))
                    self.send[mine, t] = both.astype(BF16)
                    return 0

                lax.fori_loop(0, many, pack_block, 0)
            self.copy(at).start()

    def finish(self):
        frame, rows = self.frame, self.rows
        for at, (dr, dc) in enumerate(NEIGHBOURS):
            self.incoming(at).wait()
            mine, _ = self.parts(at)
            inside = jnp.logical_and(
                jnp.logical_and(self.row + dr >= 0, self.row + dr < 32),
                jnp.logical_and(self.col + dc >= 0, self.col + dc < SIDE),
            )
            top = ROW_PAD - rows if dr < 0 else ROW_PAD + ROWS
            left = COL_PAD - 8 if dc < 0 else COL_PAD + COLS
            if dc == 0:

                def place_row(i, _, mine=mine, top=top, inside=inside):
                    line = self.recv[mine, pl.ds(i * 4, 4)].reshape(64, 128).astype(F32)
                    first, second = doubled(jnp.where(inside, line, 0.0))
                    frame[top + i, COL_PAD : COL_PAD + 64, :] = first
                    frame[top + i, COL_PAD + 64 : COL_PAD + 128, :] = second
                    return 0

                lax.fori_loop(0, rows, place_row, 0)
            else:
                base, many = (ROW_PAD, ROWS // 4) if dr == 0 else (top, rows // 4)

                def place_block(t, _, mine=mine, left=left, base=base, inside=inside):
                    block = self.recv[mine, t].astype(F32)
                    first, second = doubled(jnp.where(inside, block, 0.0))
                    frame[pl.ds(base + 4 * t, 2), left : left + 8, :] = first.reshape(2, 8, 128)
                    frame[pl.ds(base + 4 * t + 2, 2), left : left + 8, :] = second.reshape(2, 8, 128)
                    return 0

                lax.fori_loop(0, many, place_block, 0)
        for at in range(len(NEIGHBOURS)):
            self.copy(at).wait_send()


def three_taps(kernel, ky, swapped=False):
    pick = lambda kx: kernel[kx, ky] if swapped else kernel[ky, kx]
    zeros = jnp.zeros((CHAN, CHAN), BF16)
    return jnp.concatenate([pick(0), pick(1), pick(2), zeros], axis=1)


def body(
    x_ref, k1a, b1a, k1b, b1b, k2a, b2a, k2b, b2b, out_ref,
    flat, frame, slab, hidden, wide, block_y, outbox, transit, inbox,
    halo_send, halo_recv, w1a, w1b, w2a, w2b,
    halo_ss, halo_rs, ss1, rs1, ss2, rs2,
):
    row, col = lax.axis_index("row"), lax.axis_index("col")
    z, quarter = row // QUAD, lax.rem(row, QUAD)

    barrier = pltpu.get_barrier_semaphore()

    def greet(device):
        pl.semaphore_signal(barrier, inc=1, device_id=device, device_id_type=MESH)

    for dr, dc in NEIGHBOURS:
        greet((lax.rem(row + dr + 32, 32), lax.rem(col + dc + SIDE, SIDE)))

    def greet_plane(t, _):
        other = lax.rem(col + t, SIDE)
        for k in range(QUAD):

            @pl.when(jnp.logical_or(t > 0, quarter != k))
            def _():
                greet((z * QUAD + k, other))

        @pl.when(jnp.logical_or(col != z, t > 0))
        def _():
            greet((col * QUAD + quarter, other))

        return 0

    lax.fori_loop(0, SIDE, greet_plane, 0)
    waits = 8 + 31 + SIDE - jnp.where(col == z, 1, 0)

    def widen(g, _):
        flat[pl.ds(g * 256, 256), :] = x_ref[pl.ds(g * 8, 8)].astype(F32).reshape(256, 128)
        return 0

    lax.fori_loop(0, CHAN // 8, widen, 0)
    same = lax.broadcasted_iota(jnp.int32, (COLS, COLS), 0) == lax.broadcasted_iota(
        jnp.int32, (COLS, COLS), 1
    )
    unit = same.astype(F32).astype(BF16)

    def turn(i, _):
        line = flat[pl.ds(i, CHAN, stride=ROWS), :].astype(BF16)
        both = jnp.concatenate([line, line], axis=0)
        frame[ROW_PAD + i, COL_PAD : COL_PAD + COLS, :] = lax.dot_general(
            unit, both, NT, preferred_element_type=F32
        )
        return 0

    lax.fori_loop(0, ROWS, turn, 0)

    for ky in range(3):
        for target, kernel in ((w1a, k1a), (w1b, k1b)):
            taps = three_taps(kernel, ky)
            target[:, ky * 256 : ky * 256 + 256] = jnp.concatenate([taps, taps], axis=0)
        w2a[:, ky * 256 : ky * 256 + 256] = jnp.concatenate(
            [three_taps(k2a, ky), three_taps(k2a, ky, True)], axis=0
        )
        for kx in range(3):
            zeros = jnp.zeros((CHAN, CHAN), BF16)
            upper = jnp.concatenate([k2b[ky, kx], zeros], axis=1)
            lower = jnp.concatenate([zeros, k2b[kx, ky]], axis=1)
            at = ky * 384 + kx * 128
            w2b[:, at : at + 128] = jnp.concatenate([upper, lower], axis=0)

    def bias(ref):
        return jnp.concatenate([ref[...], ref[...]], axis=1)

    def within(first_row, count):
        shape = (count, 144, 128)
        i = lax.broadcasted_iota(jnp.int32, shape, 0) + (first_row + row * ROWS)
        j = lax.broadcasted_iota(jnp.int32, shape, 1) + (col * COLS - HID_COL)
        full = jnp.logical_and(i >= 0, i < 32 * ROWS)
        return jnp.logical_and(full, jnp.logical_and(j >= 0, j < SIDE * COLS))

    pl.semaphore_wait(barrier, waits)

    halo = Halo(4, frame, halo_send.at[0], halo_recv.at[0], halo_ss.at[0], halo_rs.at[0], row, col)
    halo.start()
    halo.finish()

    def shifted(d, top):
        def one(i, _):
            at = COL_PAD - HID_COL
            left = frame[top + i, at - d : at - d + 144, :]
            here = frame[top + i, at : at + 144, :]
            right = frame[top + i, at + d : at + d + 144, :]
            slab[top + i, :, 0:128] = paired(left, here).astype(BF16)
            slab[top + i, :, 128:256] = right.astype(BF16)
            return 0

        return one

    def conv_a(d, weights, bias_ref, step):
        def one(t, _):
            i = t * step - d
            lhs = jnp.concatenate(
                [
                    slab[pl.ds(i + ROW_PAD + (ky - 1) * d, step)].reshape(step * 144, 256)
                    for ky in range(3)
                ],
                axis=1,
            )
            total = lax.dot_general(lhs, weights[...], NT, preferred_element_type=F32)
            value = rounded(elu(total + bias(bias_ref))).reshape(step, 144, 128)
            hidden[pl.ds(i + HID_ROW, step)] = jnp.where(within(i, step), value, 0.0)
            return 0

        return one

    lax.fori_loop(0, 40, shifted(2, ROW_PAD - 4), 0)
    lax.fori_loop(0, 9, conv_a(2, w1a, b1a, 4), 0)

    def hidden_taps(i, _):
        at = i + HID_ROW - 2
        left = hidden[at, HID_COL - 2 : HID_COL + 126, :]
        here = hidden[at, HID_COL : HID_COL + 128, :]
        right = hidden[at, HID_COL + 2 : HID_COL + 130, :]
        slab[i, 0:128, 0:128] = paired(left, here).astype(BF16)
        slab[i, 0:128, 128:256] = right.astype(BF16)
        return 0

    lax.fori_loop(0, 36, hidden_taps, 0)

    def conv_b_one(t, _):
        i = t * 4
        lhs = jnp.concatenate(
            [slab[pl.ds(i + 2 * ky, 4), 0:128, :].reshape(512, 256) for ky in range(3)], axis=1
        )
        total = lax.dot_general(lhs, w1b[...], NT, preferred_element_type=F32)
        here = frame[pl.ds(ROW_PAD + i, 4), COL_PAD : COL_PAD + COLS, :].reshape(512, 128)
        block_y[pl.ds(i * COLS, 512), :] = rounded(elu(here + total + bias(b1b)))
        return 0

    lax.fori_loop(0, ROWS // 4, conv_b_one, 0)

    def spread(t, _):
        via = lax.rem(col + 1 + t, SIDE)
        for k in range(QUAD):
            for u in range(4):
                column = block_y[pl.ds(32 * k + 4 * via + u, ROWS, stride=COLS), :]
                outbox[via, k, u] = paired(column[:16], column[16:]).astype(BF16)
            alone = jnp.logical_and(t == SIDE - 1, quarter == k)

            @pl.when(alone)
            def _():
                pltpu.make_async_copy(
                    outbox.at[via, k], transit.at[col, quarter], rs1.at[col]
                ).start()

            @pl.when(jnp.logical_not(alone))
            def _():
                pltpu.make_async_remote_copy(
                    outbox.at[via, k],
                    transit.at[col, quarter],
                    ss1,
                    rs1.at[col],
                    device_id=(z * QUAD + k, via),
                    device_id_type=MESH,
                ).start()

        return 0

    lax.fori_loop(0, SIDE, spread, 0)

    def forward(t, _):
        origin = lax.rem(col + 2 * SIDE - 1 - t, SIDE)
        pltpu.make_async_copy(transit.at[origin], transit.at[origin], rs1.at[origin]).wait()
        alone = jnp.logical_and(origin == z, col == z)

        @pl.when(alone)
        def _():
            pltpu.make_async_copy(transit.at[origin], inbox.at[col], rs2.at[col]).start()

        @pl.when(jnp.logical_not(alone))
        def _():
            pltpu.make_async_remote_copy(
                transit.at[origin],
                inbox.at[col],
                ss2,
                rs2.at[col],
                device_id=(origin * QUAD + quarter, z),
                device_id_type=MESH,
            ).start()

        return 0

    lax.fori_loop(0, SIDE, forward, 0)

    def arrive(t, _):
        via = lax.rem(z + 1 + t, SIDE)
        pltpu.make_async_copy(inbox.at[via], inbox.at[via], rs2.at[via]).wait()
        for u in range(4):
            i = via * 4 + u
            for k in range(QUAD):
                mirror = doubled(inbox[via, k, u].astype(F32))
                for half in range(2):
                    j = 32 * k + 16 * half
                    own = block_y[pl.ds(pl.multiple_of(i * COLS + j, 16), 16), :]
                    frame[ROW_PAD + i, COL_PAD + j : COL_PAD + j + 16, :] = rounded(
                        (own + mirror[half]) * 0.5
                    )
        return 0

    lax.fori_loop(0, SIDE, arrive, 0)

    halo = Halo(8, frame, halo_send.at[1], halo_recv.at[1], halo_ss.at[1], halo_rs.at[1], row, col)
    halo.start()
    halo.finish()

    lax.fori_loop(0, 48, shifted(4, 0), 0)
    lax.fori_loop(0, 10, conv_a(4, w2a, b2a, 4), 0)

    def wide_taps(i, _):
        for kx in range(3):
            at = HID_COL + 4 * (kx - 1)
            wide[i, :, kx * 128 : kx * 128 + 128] = hidden[i, at : at + 128, :].astype(BF16)
        return 0

    lax.fori_loop(0, 40, wide_taps, 0)

    lane = lax.broadcasted_iota(jnp.int32, (CHAN, 128), 1)
    chan = lax.broadcasted_iota(jnp.int32, (CHAN, 128), 0)
    mean = jnp.where(jnp.logical_or(lane == chan, lane == chan + CHAN), 0.5, 0.0).astype(BF16)

    def conv_b_two(t, _):
        i = t * 4
        lhs = jnp.concatenate(
            [wide[pl.ds(i + 4 * ky, 4)].reshape(512, 384) for ky in range(3)], axis=1
        )
        total = lax.dot_general(lhs, w2b[...], NT, preferred_element_type=F32)
        here = frame[pl.ds(ROW_PAD + i, 4), COL_PAD : COL_PAD + COLS, :].reshape(512, 128)
        both = elu(here + total + bias(b2b)).astype(BF16)
        for u in range(4):
            line = both[u * COLS : (u + 1) * COLS]
            flat[pl.ds(i + u, CHAN, stride=ROWS), :] = lax.dot_general(
                mean, line, NT, preferred_element_type=F32
            )
        return 0

    lax.fori_loop(0, ROWS // 4, conv_b_two, 0)

    def narrow(g, _):
        out_ref[pl.ds(g * 8, 8)] = flat[pl.ds(g * 256, 256), :].reshape(8, ROWS, COLS).astype(BF16)
        return 0

    lax.fori_loop(0, CHAN // 8, narrow, 0)

    def sent_one(t, _):
        for k in range(QUAD):

            @pl.when(jnp.logical_not(jnp.logical_and(t == SIDE - 1, quarter == k)))
            def _():
                pltpu.make_async_copy(outbox.at[0, 0], outbox.at[0, 0], ss1).wait()

        @pl.when(jnp.logical_or(t > 0, col != z))
        def _():
            pltpu.make_async_copy(transit.at[0], transit.at[0], ss2).wait()

        return 0

    lax.fori_loop(0, SIDE, sent_one, 0)


def shards(pair_map, k1a, b1a, k1b, b1b, k2a, b2a, k2b, b2b):
    wide = lambda b: b.reshape(1, CHAN)
    vmem = pl.BlockSpec(memory_space=pltpu.VMEM)
    dma, regular = pltpu.SemaphoreType.DMA, pltpu.SemaphoreType.REGULAR
    return pl.pallas_call(
        body,
        out_shape=jax.ShapeDtypeStruct((CHAN, ROWS, COLS), BF16),
        in_specs=[vmem] * 9,
        out_specs=vmem,
        scratch_shapes=[
            pltpu.VMEM((CHAN * ROWS, COLS), F32),
            pltpu.VMEM((ROWS + 2 * ROW_PAD, COLS + 2 * COL_PAD, 128), F32),
            pltpu.VMEM((ROWS + 2 * ROW_PAD, 144, 256), BF16),
            pltpu.VMEM((ROWS + 2 * HID_ROW, 144, 128), F32),
            pltpu.VMEM((ROWS + 2 * HID_ROW, COLS, 384), BF16),
            pltpu.VMEM((ROWS * COLS, 128), F32),
            pltpu.VMEM((SIDE, QUAD, 4, 16, 128), BF16),
            pltpu.VMEM((SIDE, QUAD, 4, 16, 128), BF16),
            pltpu.VMEM((SIDE, QUAD, 4, 16, 128), BF16),
            pltpu.VMEM((2, 8, 32, 16, 128), BF16),
            pltpu.VMEM((2, 8, 32, 16, 128), BF16),
            pltpu.VMEM((128, 768), BF16),
            pltpu.VMEM((128, 768), BF16),
            pltpu.VMEM((128, 768), BF16),
            pltpu.VMEM((128, 1152), BF16),
            dma((2, 8)),
            dma((2, 8)),
            dma,
            dma((SIDE,)),
            dma,
            dma((SIDE,)),
        ],
        compiler_params=pltpu.CompilerParams(
            collective_id=0, has_side_effects=True, vmem_limit_bytes=50 << 20
        ),
    )(pair_map, k1a, wide(b1a), k1b, wide(b1b), k2a, wide(b2a), k2b, wide(b2b))


def solution(mesh):
    placed = (P(None, "row", "col"), P(), P(), P(), P(), P(), P(), P(), P())
    return jax.shard_map(
        shards, mesh=mesh, in_specs=placed, out_specs=P(None, "row", "col"), check_vma=False
    )
```

time: 246 us -> 80.1 us (0.33)
  the two profiles are of different devices: /device:TPU:1 before, /device:TPU:80 now
where the time goes in v1:
time: 80.1 us; the launch traced here: 79.9 us
  Pallas kernels  73.7 us (92%)
  local copies, waits for them, and re-layouts  6.16 us (8%)
    pallas_call x1, Pallas kernels, shards(): pl.pallas_call(body, out_shape=jax.ShapeDtypeStruct((CHAN, ROWS, COLS), B...  73.7 us
    unnamed x19, local copies, waits for them, and re-layouts  6.16 us

profile of v1, /device:TPU:80, one launch (start us, length us, event | category | flops | bytes accessed | tf_op | source)
XLA Modules:
  0.0 79.9 jit_solution(7139256919501053033)
XLA Ops:
  0.0 0.0 copy-start.8
  0.0 0.0 copy-start.5
  0.0 0.0 copy-start.6
  0.0 0.0 copy-start.7
  0.0 0.6 copy-done.8
  0.7 0.0 copy-done.5
  0.7 0.0 copy-done.6
  0.7 0.0 copy-done.7
  0.7 0.0 copy-start
  0.7 1.0 %copy-done = bf16[64,32,128]{2,1,0:T(8,128)(2,1)S(1)} copy-done((bf16[64,32,128]{2,1,0:T(8,128)(2,1)S(1)}, bf16[64,32,128]{2,1,0:T(8,128)(2,1)}, u32[]{:S(2)}) %copy-start) | copy-done | bytes 524312
  1.7 0.0 copy-start.1
  1.7 0.9 %copy-done.1 = bf16[3,3,64,64]{3,2,1,0:T(8,128)(2,1)S(1)} copy-done((bf16[3,3,64,64]{3,2,1,0:T(8,128)(2,1)S(1)}, bf16[3,3,64,64]{3,2,1,0:T(8,128)(2,1)}, u32[]{:S(2)}) %copy-start.1) | copy-done | bytes 73752
  2.7 0.0 copy-start.2
  2.7 0.9 %copy-done.2 = bf16[3,3,64,64]{3,2,1,0:T(8,128)(2,1)S(1)} copy-done((bf16[3,3,64,64]{3,2,1,0:T(8,128)(2,1)S(1)}, bf16[3,3,64,64]{3,2,1,0:T(8,128)(2,1)}, u32[]{:S(2)}) %copy-start.2) | copy-done | bytes 73752
  3.6 0.0 copy-start.3
  3.6 0.9 %copy-done.3 = bf16[3,3,64,64]{3,2,1,0:T(8,128)(2,1)S(1)} copy-done((bf16[3,3,64,64]{3,2,1,0:T(8,128)(2,1)S(1)}, bf16[3,3,64,64]{3,2,1,0:T(8,128)(2,1)}, u32[]{:S(2)}) %copy-start.3) | copy-done | bytes 73752
  4.5 0.0 copy-start.4
  4.5 0.9 %copy-done.4 = bf16[3,3,64,64]{3,2,1,0:T(8,128)(2,1)S(1)} copy-done((bf16[3,3,64,64]{3,2,1,0:T(8,128)(2,1)S(1)}, bf16[3,3,64,64]{3,2,1,0:T(8,128)(2,1)}, u32[]{:S(2)}) %copy-start.4) | copy-done | bytes 73752
  5.4 73.7 %shard_map.91 = bf16[64,32,128]{2,1,0:T(8,128)(2,1)S(1)} custom-call(bf16[64,32,128]{2,1,0:T(8,128)(2,1)S(1)} %copy-done, bf16[3,3,64,64]{3,2,1,0:T(8,128)(2,1)S(1)} %copy-done.1, f32[1,64]{1,0:T(1,128)S(1)} %bitcast.4, bf16[3,3,64,64]{3,2,1,0:T(8,128)(2,1)S(1)} %copy-done.2, f32[1,64]{1,0:T(1,128)S(1)} %bitcast.5, bf16[3,3,64,64]{3,2,1,0:T(8,128)(2,1)S(1)} %copy-done.3, ...), custom_call_target="tpu_custom_call" | custom-call | tf_op jit(solution)/shard_map/pallas_call | solution.py:415
  79.1 0.8 copy.11
Async XLA Ops:
  0.0 0.7 copy-start.8
  0.0 0.7 copy-start.5
  0.0 0.7 copy-start.6
  0.0 0.7 copy-start.7
  0.7 1.0 %copy-start = (bf16[64,32,128]{2,1,0:T(8,128)(2,1)S(1)}, bf16[64,32,128]{2,1,0:T(8,128)(2,1)}, u32[]{:S(2)}) copy-start(bf16[64,32,128]{2,1,0:T(8,128)(2,1)} %x_ref.1) | copy-start | bytes 1572868
  1.7 0.9 %copy-start.1 = (bf16[3,3,64,64]{3,2,1,0:T(8,128)(2,1)S(1)}, bf16[3,3,64,64]{3,2,1,0:T(8,128)(2,1)}, u32[]{:S(2)}) copy-start(bf16[3,3,64,64]{3,2,1,0:T(8,128)(2,1)} %k1a.1) | copy-start | bytes 221188
  2.7 0.9 %copy-start.2 = (bf16[3,3,64,64]{3,2,1,0:T(8,128)(2,1)S(1)}, bf16[3,3,64,64]{3,2,1,0:T(8,128)(2,1)}, u32[]{:S(2)}) copy-start(bf16[3,3,64,64]{3,2,1,0:T(8,128)(2,1)} %k1b.1) | copy-start | bytes 221188
  3.6 0.9 %copy-start.3 = (bf16[3,3,64,64]{3,2,1,0:T(8,128)(2,1)S(1)}, bf16[3,3,64,64]{3,2,1,0:T(8,128)(2,1)}, u32[]{:S(2)}) copy-start(bf16[3,3,64,64]{3,2,1,0:T(8,128)(2,1)} %k2a.1) | copy-start | bytes 221188
  4.5 0.9 %copy-start.4 = (bf16[3,3,64,64]{3,2,1,0:T(8,128)(2,1)S(1)}, bf16[3,3,64,64]{3,2,1,0:T(8,128)(2,1)}, u32[]{:S(2)}) copy-start(bf16[3,3,64,64]{3,2,1,0:T(8,128)(2,1)} %k2b.1) | copy-start | bytes 221188
